TPU v7x, 32 devices: a whole 2x2x4 slice. The times are simulated.
32 devices in a mesh: rows: 16 (over z, y, core), tp: 2 (over x).
Axes of the slice: x: 2, y: 2, z: 4, core: 2. Of those that a mesh axis runs over, the one named last changes fastest.
Arguments:
- normed_rows: bfloat16 [4096, 8192], P('rows'), may hold values from -6 to 6
- value_weight: bfloat16 [8192, 1024], P(None, 'tp'), may hold values from -0.0625 to 0.0625
- adapter_a: bfloat16 [32, 8192, 64], P('rows', 'tp'), may hold values from -0.0625 to 0.0625
- adapter_b: bfloat16 [32, 64, 1024], P('rows', None, 'tp'), may hold values from -0.75 to 0.75
- page_table: int32 [32], replicated, may hold values from 0 to 31, as said below
- group_list: int32 [16, 16], replicated, may hold values from 0 to 31, as said below
- seg_len: int32 [16, 16], P('rows'), may hold values from 1 to 32, 256 in all within a row
- kv_len: int32 [16, 256], P('rows'), may hold values from 1 to 32, 4096 in all within a row
- queries: bfloat16 [4096, 8192], P('rows', 'tp'), may hold values from -8 to 8
- new_key: bfloat16 [4096, 1024], P('rows', 'tp'), may hold values from -8 to 8
- cache_keys: bfloat16 [4096, 32, 1024], P('rows', None, 'tp'), may hold values from -8 to 8
- cache_values: bfloat16 [4096, 32, 1024], P('rows', None, 'tp'), may hold values from -6 to 6
Outputs:
- new_value: bfloat16 [4096, 1024], P('rows', 'tp')
- attended: bfloat16 [4096, 8192], P('rows', 'tp')
Inputs may be any that keep to these rules, and one draw needn't show every extreme that they name: `page_table`: each adapter has one position; the device of rows index p // 2 stores position p. `group_list`: the 16 adapters of a group are stored on 16 different indices of rows.
All inputs are finite; a program needn't handle non-finite values.
Results may differ from a plain program's by a relative error of at most 0.0048.
Values may be sent and summed in bfloat16 or wider, within the bound.
A program may use at most 128 MiB of HBM per device.

v0:
```python
import math

import jax
import jax.numpy as jnp
from jax import lax
from jax.sharding import PartitionSpec as P

HEAD = 128


def cache_scores(q_four, k_four, lengths, scale):
    score = (
        jnp.einsum("rhgd,rchd->rhgc", q_four, k_four, preferred_element_type=jnp.float32) * scale
    )
    valid = (jnp.arange(k_four.shape[1], dtype=jnp.int32)[None, :] < lengths[:, None])[
        :, None, None, :
    ]
    return (score, valid)


def body(
    normed_rows,
    value_weight,
    adapter_a,
    adapter_b,
    page_table,
    group_list,
    seg_len,
    kv_len,
    queries,
    new_key,
    cache_keys,
    cache_values,
):
    tp_index = lax.axis_index("tp")
    groups = lax.axis_size("rows")
    own_group = lax.axis_index("rows")
    rows_count = normed_rows.shape[0]
    part = normed_rows.shape[1] // lax.axis_size("tp")
    per_owner = adapter_a.shape[0]
    adapters_count = page_table.shape[0]
    lens = seg_len[0]
    slots = lens.shape[0]
    most = 2 * rows_count // slots
    heads_kv = new_key.shape[1] // HEAD
    group = queries.shape[1] // new_key.shape[1]
    scale = 1.0 / math.sqrt(HEAD)
    lengths = kv_len[0]
    q_four = queries.reshape(rows_count, heads_kv, group, HEAD)
    k_four = cache_keys.reshape(rows_count, -1, heads_kv, HEAD)
    v_four = cache_values.reshape(rows_count, -1, heads_kv, HEAD)
    k_own = new_key.reshape(rows_count, heads_kv, HEAD)
    x_part = lax.dynamic_slice_in_dim(normed_rows, tp_index * part, part, 1)
    ends = jnp.cumsum(lens)
    starts = ends - lens
    rowpos = jnp.arange(rows_count, dtype=jnp.int32)
    segment = jnp.sum((rowpos[:, None] >= ends[None, :]).astype(jnp.int32), axis=1)
    in_segment = segment[:, None] == jnp.arange(slots, dtype=jnp.int32)[None, :]
    within = rowpos - jnp.sum(jnp.where(in_segment, starts[None, :], 0), axis=1)
    listed = group_list.reshape(-1)
    positions = jnp.sum(
        jnp.where(
            listed[:, None] == jnp.arange(adapters_count, dtype=jnp.int32)[None, :],
            page_table[None, :],
            0,
        ),
        axis=1,
    ).reshape(groups, slots)
    owners = positions // per_owner
    my_owners = lax.dynamic_index_in_dim(owners, own_group, 0, keepdims=False)
    owner_of_row = jnp.sum(jnp.where(in_segment, my_owners[None, :], 0), axis=1)
    target = owner_of_row * most + within
    placing = (jnp.arange(groups * most, dtype=jnp.int32)[:, None] == target[None, :]).astype(
        jnp.bfloat16
    )
    placed_rows = (
        jnp.dot(placing, x_part, preferred_element_type=jnp.float32)
        .astype(jnp.bfloat16)
        .reshape(groups, most, part)
    )
    mine = owners == own_group
    local = positions % per_owner
    hits = mine[:, :, None] & (
        local[:, :, None] == jnp.arange(per_owner, dtype=jnp.int32)[None, None, :]
    )
    selector = jnp.sum(hits.astype(jnp.float32), axis=1)
    arrived = lax.all_to_all(placed_rows, "rows", split_axis=0, concat_axis=0, tiled=True)
    low_each = jnp.einsum("nmd,jdr->njmr", arrived, adapter_a, preferred_element_type=jnp.float32)
    low_part = jnp.sum(low_each * selector[:, :, None, None], axis=1)
    low = lax.psum(low_part, "tp").astype(jnp.bfloat16)
    delta_each = jnp.einsum("nmr,jrk->njmk", low, adapter_b, preferred_element_type=jnp.float32)
    delta_out = jnp.sum(delta_each * selector[:, :, None, None], axis=1).astype(jnp.bfloat16)
    delta = lax.all_to_all(delta_out, "rows", split_axis=0, concat_axis=0, tiled=True)
    delta_rows = lax.dot_general(
        placing,
        delta.reshape(groups * most, -1),
        (((0,), (0,)), ((), ())),
        preferred_element_type=jnp.float32,
    )
    base = jnp.dot(normed_rows, value_weight, preferred_element_type=jnp.float32)
    new_value = (base + delta_rows).astype(jnp.bfloat16)
    v_own = new_value.reshape(rows_count, heads_kv, HEAD)
    k_joined = jnp.concatenate([k_four, k_own[:, None]], axis=1)
    v_joined = jnp.concatenate([v_four, v_own[:, None]], axis=1)
    score, valid = cache_scores(q_four, k_joined, lengths, scale)
    valid = (
        valid
        | (jnp.arange(k_joined.shape[1], dtype=jnp.int32) == k_joined.shape[1] - 1)[
            None, None, None, :
        ]
    )
    top = jnp.max(jnp.where(valid, score, -jnp.inf), axis=-1)
    expd = jnp.where(valid, jnp.exp(score - top[..., None]), 0.0)
    total = jnp.sum(expd, axis=-1)
    context = jnp.einsum(
        "rhgc,rchd->rhgd", expd.astype(jnp.bfloat16), v_joined, preferred_element_type=jnp.float32
    )
    attended = (context / total[..., None]).astype(jnp.bfloat16).reshape(rows_count, -1)
    return (new_value, attended)


def solution(mesh):
    return jax.shard_map(
        body,
        mesh=mesh,
        in_specs=(
            P("rows", None),
            P(None, "tp"),
            P("rows", "tp", None),
            P("rows", None, "tp"),
            P(),
            P(),
            P("rows", None),
            P("rows", None),
            P("rows", "tp"),
            P("rows", "tp"),
            P("rows", None, "tp"),
            P("rows", None, "tp"),
        ),
        out_specs=(P("rows", "tp"), P("rows", "tp")),
        check_vma=False,
    )
```

profile of v0, /device:TPU:0, one launch (start us, length us, event | category | flops | bytes accessed | tf_op | source)
XLA Modules:
  0.0 182.1 jit_solution(12620933013410154905)
XLA Ops:
  0.6 0.0 copy-start
  0.7 0.9 eq.80
  1.5 0.7 select_reduce_fusion.1
  2.3 0.1 reshape.142
  2.4 0.7 copy.24
  3.1 0.1 reduce.3
  3.2 0.1 convert_reduce_fusion.1
  3.3 0.7 fusion.38
  4.0 0.1 select_reduce_fusion.3
  4.1 4.8 %convolution_convert_fusion = bf16[512,4096]{1,0:T(8,128)(2,1)} fusion(bf16[256,8192]{1,0:T(8,128)(2,1)} %param.12, s32[]{:T(128)S(6)} %select_n.54, s32[256]{0:T(256)S(1)} %subtract_add_fusion), kind=kOutput, calls=%fused_computation.9 | convolution fusion | flops 1075970048 | bytes 6292484 | tf_op jit(solution)/shard_map/dot_general | solution.py:77
  8.9 7.4 %all-to-all-start = ((bf16[16,32,4096]{2,1,0:T(8,128)(2,1)}), bf16[16,32,4096]{2,1,0:T(8,128)(2,1)}, u32[]{:S(2)}, u32[]{:S(2)}) async-start(bf16[16,32,4096]{2,1,0:T(8,128)(2,1)} %bitcast.58), calls=%async_computation | async-start | bytes 8388608 | tf_op jit(solution)/shard_map/all_to_all | solution.py:87
  16.4 0.1 convert_reduce_fusion
  16.5 0.1 copy.25
  16.6 13.7 %copy.27 = bf16[256,32,512]{0,2,1:T(8,128)(2,1)} copy(bf16[256,32,512]{2,1,0:T(8,128)(2,1)} %param.22) | data formatting | bytes 16777216 | tf_op args[10]
  30.3 0.0 copy-start.2
  30.3 14.8 %copy.29 = bf16[256,32,4,128]{3,1,2,0:T(8,128)(2,1)} copy(bf16[256,32,4,128]{0,3,2,1:T(8,128)(2,1)} %bitcast.56) | data formatting | bytes 16777216 | tf_op jit(solution)/shard_map/reshape | solution.py:50
  45.1 0.0 copy-start.4
  45.1 0.0 copy-start.5
  45.1 0.0 copy-done.2
  45.1 1.8 copy.36
  46.9 0.0 copy-done.4
  46.9 0.1 copy.28
  47.1 0.4 copy.30
  47.5 0.0 copy-done.5
  47.5 0.1 fusion.34
  47.6 11.5 %fusion.1 = f32[256,4,33,8]{2,3,1,0:T(8,128)} fusion(bf16[256,4,8,128]{3,2,1,0:T(8,128)(2,1)} %bitcast.61, bf16[256,1,4,128]{3,1,2,0:T(2,128)(2,1)S(1)} %copy.30, bf16[256,32,4,128]{3,1,2,0:T(8,128)(2,1)} %copy.29), kind=kOutput, calls=%fused_computation.1 | convolution fusion | flops 86507520 | bytes 11829248 | tf_op jit(solution)/shard_map/rhgd,rchd->rhgc/dot_general | solution.py:13
  59.1 0.0 copy-start.6
  59.1 34.9 %all-to-all-done = bf16[16,32,4096]{2,1,0:T(8,128)(2,1)} async-done(((bf16[16,32,4096]{2,1,0:T(8,128)(2,1)}), bf16[16,32,4096]{2,1,0:T(8,128)(2,1)}, u32[]{:S(2)}, u32[]{:S(2)}) %all-to-all-start) | async-done | bytes 4194336 | tf_op jit(solution)/shard_map/all_to_all | solution.py:87
  94.0 0.0 copy-done
  94.0 3.5 %fusion.23 = f32[16,32,64]{2,1,0:T(8,128)S(1)} fusion(bf16[16,32,4096]{2,1,0:T(8,128)(2,1)} %all-to-all-done, bf16[2,4096,64]{1,2,0:T(8,128)(2,1)S(1)} %copy-done, f32[16,2]{1,0:T(8,128)S(1)} %copy.25), kind=kOutput, calls=%fused_computation.28 | convolution fusion | flops 536969216 | bytes 5374080 | tf_op jit(solution)/shard_map/nmd,jdr->njmr/dot_general | solution.py:88
  97.5 13.1 %all-reduce.1 = bf16[16,32,64]{2,1,0:T(8,128)(2,1)S(1)} all-reduce(f32[16,32,64]{2,1,0:T(8,128)S(1)} %fusion.23), channel_id=1, replica_groups=mesh['rows'=16,'tp'=2] {'tp'}, use_global_device_ids=true, to_apply=%region_7.8 | all-reduce | flops 32768 | bytes 196608 | tf_op jit(solution)/shard_map/psum | solution.py:90
  110.6 0.0 copy-done.6
  110.6 1.2 multiply_reduce_fusion
  111.8 18.8 %all-to-all-start.1 = ((bf16[16,32,512]{2,1,0:T(8,128)(2,1)}), bf16[16,32,512]{2,1,0:T(8,128)(2,1)S(1)}, u32[]{:S(2)}, u32[]{:S(2)}) async-start(bf16[16,32,512]{2,1,0:T(8,128)(2,1)} %multiply_reduce_fusion), calls=%async_computation.1 | async-start | bytes 1048576 | tf_op jit(solution)/shard_map/all_to_all | solution.py:93
  130.6 7.4 %bitcast_reduce_fusion = (f32[256,4,8]{2,1,0:T(4,128)S(1)}, bf16[256,4,33,8]{2,3,1,0:T(8,128)(2,1)}) fusion(f32[256,4,33,8]{2,3,1,0:T(8,128)} %fusion.1, pred[256,33]{1,0:T(8,128)(4,1)S(1)} %fusion.34), kind=kOutput, calls=%fused_computation.12 | output fusion | flops 1892384 | bytes 1663232 | tf_op jit(solution)/shard_map/sub | solution.py:113
  138.0 13.7 %copy.31 = bf16[256,32,512]{0,2,1:T(8,128)(2,1)} copy(bf16[256,32,512]{2,1,0:T(8,128)(2,1)} %param.23) | data formatting | bytes 16777216 | tf_op args[11]
  151.7 14.7 %copy.32 = bf16[256,32,4,128]{3,1,2,0:T(8,128)(2,1)} copy(bf16[256,32,4,128]{0,3,2,1:T(8,128)(2,1)} %bitcast.57) | data formatting | bytes 16777216 | tf_op jit(solution)/shard_map/reshape | solution.py:51
  166.4 7.0 %fusion.46 = f32[256,512]{1,0:T(8,128)S(1)} fusion(bf16[256,8192]{1,0:T(8,128)(2,1)} %param.12, bf16[8192,512]{1,0:T(8,128)(2,1)} %param.13), kind=kOutput, calls=%fused_computation.68 | convolution fusion | flops 2147483648 | bytes 13107200 | tf_op jit(solution)/shard_map/dot_general | solution.py:100
  173.4 0.0 all-to-all-done.1
  173.4 0.4 fusion.22
  173.8 0.0 copy-start.3
  173.8 0.2 broadcast_in_dim_reshape.9
  173.9 0.0 copy-start.1
  174.0 5.9 %divide_convert_fusion = bf16[256,4,8,128]{3,2,1,0:T(8,128)(2,1)S(1)} fusion(f32[256,4,8]{2,1,0:T(4,128)S(1)} %get-tuple-element.6, bf16[256,1,4,128]{3,1,2,0:T(2,128)(2,1)S(1)} %broadcast_in_dim_reshape.9, bf16[256,32,4,128]{3,1,2,0:T(8,128)(2,1)} %copy.32, bf16[256,4,33,8]{2,3,1,0:T(8,128)(2,1)} %get-tuple-element.7), kind=kOutput, calls=%fused_computation.14 | convolution fusion | flops 88604672 | bytes 11321344 | tf_op jit(solution)/shard_map/rhgc,rchd->rhgd/dot_general | solution.py:115
  179.8 0.0 copy-done.3
  179.8 2.3 %copy.39 = bf16[32,8,32,128]{3,1,2,0:T(8,128)(2,1)} copy(bf16[32,8,32,128]{3,2,1,0:T(8,128)(2,1)S(1)} %bitcast.62) | data formatting | bytes 4194304
  182.1 0.0 copy-done.1
  (5 shorter events, 0.1 us)
Async XLA Ops:
  0.6 93.4 %copy-start = (bf16[2,4096,64]{1,2,0:T(8,128)(2,1)S(1)}, bf16[2,4096,64]{1,2,0:T(8,128)(2,1)}, u32[]{:S(2)}) copy-start(bf16[2,4096,64]{1,2,0:T(8,128)(2,1)} %param.14) | copy-start | bytes 3145732
  8.9 85.1 %all-to-all-start = ((bf16[16,32,4096]{2,1,0:T(8,128)(2,1)}), bf16[16,32,4096]{2,1,0:T(8,128)(2,1)}, u32[]{:S(2)}, u32[]{:S(2)}) async-start(bf16[16,32,4096]{2,1,0:T(8,128)(2,1)} %bitcast.58), calls=%async_computation | async-start | bytes 8388608 | tf_op jit(solution)/shard_map/all_to_all | solution.py:87
  30.3 14.8 %copy-start.2 = (bf16[256,4096]{1,0:T(8,128)(2,1)S(1)}, bf16[256,4096]{1,0:T(8,128)(2,1)}, u32[]{:S(2)}) copy-start(bf16[256,4096]{1,0:T(8,128)(2,1)} %param.20) | copy-start | bytes 6291460
  45.1 1.8 copy-start.4
  45.1 2.4 %copy-start.5 = (s32[1,256]{1,0:T(1,128)S(1)}, s32[1,256]{1,0:T(1,128)}, u32[]{:S(2)}) copy-start(s32[1,256]{1,0:T(1,128)} %param.19) | copy-start | bytes 3076
  59.1 51.5 %copy-start.6 = (bf16[2,64,512]{2,1,0:T(8,128)(2,1)S(1)}, bf16[2,64,512]{2,1,0:T(8,128)(2,1)}, u32[]{:S(2)}) copy-start(bf16[2,64,512]{2,1,0:T(8,128)(2,1)} %param.15) | copy-start | bytes 393220
  111.8 61.5 %all-to-all-start.1 = ((bf16[16,32,512]{2,1,0:T(8,128)(2,1)}), bf16[16,32,512]{2,1,0:T(8,128)(2,1)S(1)}, u32[]{:S(2)}, u32[]{:S(2)}) async-start(bf16[16,32,512]{2,1,0:T(8,128)(2,1)} %multiply_reduce_fusion), calls=%async_computation.1 | async-start | bytes 1048576 | tf_op jit(solution)/shard_map/all_to_all | solution.py:93
  173.8 6.1 %copy-start.3 = (bf16[256,512]{1,0:T(8,128)(2,1)}, bf16[256,512]{1,0:T(8,128)(2,1)S(1)}, u32[]{:S(2)}) copy-start(bf16[256,512]{1,0:T(8,128)(2,1)S(1)} %fusion.22) | copy-start | bytes 786436
  173.9 8.2 %copy-start.1 = (bf16[2,4096,64]{1,2,0:T(8,128)(2,1)S(1)}, bf16[2,4096,64]{1,2,0:T(8,128)(2,1)}, u32[]{:S(2)}) copy-start(bf16[2,4096,64]{1,2,0:T(8,128)(2,1)} %param.14) | copy-start | bytes 3145732
where the time goes:
time: 184 us; the launch traced here: 182 us
  local copies, waits for them, and re-layouts  63.6 us (35%)
  waiting for transfers between devices  34.9 us (19%)
  matrix products  34.2 us (19%)
  starting transfers between devices  26.2 us (14%)
  blocking collectives  13.1 us (7%)
  other arithmetic  9.33 us (5%)
    all_to_all x1, waiting for transfers between devices, body(): lax.all_to_all(placed_rows, 'rows', split_axis=0, concat_axis=0, tiled=True)  34.9 us
    unnamed x19, local copies, waits for them, and re-layouts  31.7 us
    all_to_all x1, starting transfers between devices, body(): lax.all_to_all(delta_out, 'rows', split_axis=0, concat_axis=0, tiled=True)  18.8 us
    reshape x1, local copies, waits for them, and re-layouts, body(): k_four = cache_keys.reshape(rows_count, -1, heads_kv, HEAD)  14.8 us
    reshape x1, local copies, waits for them, and re-layouts, body(): v_four = cache_values.reshape(rows_count, -1, heads_kv, HEAD)  14.7 us
    psum x1, blocking collectives, body(): low = lax.psum(low_part, 'tp').astype(jnp.bfloat16)  13.1 us
    dot_general x1, matrix products, cache_scores(): jnp.einsum('rhgd,rchd->rhgc', q_four, k_four, preferred_element_type=jnp....  11.5 us
    all_to_all x1, starting transfers between devices, body(): lax.all_to_all(placed_rows, 'rows', split_axis=0, concat_axis=0, tiled=True)  7.44 us
  transfers between devices with their start and end apart: 2, of which 1 were waited for; matrix products, arithmetic and copies ran while one was open for 47% of the time, Pallas kernels for 0%

commit v1 on v0

v1 whole, which is shorter than its diff:
```python
import functools
import math

import jax
import jax.numpy as jnp
from jax import lax
from jax.experimental import pallas as pl
from jax.experimental.pallas import tpu as pltpu
from jax.sharding import Mesh, PartitionSpec as P

HEAD = 128
BLOCK = 16
OFF = -1e30


def attend_kernel(heads_kv, group, scale, q_ref, kn_ref, k_ref, v_ref, col_ref, diag_ref, ctx_ref, own_ref):
    rows = q_ref.shape[0]
    cache = k_ref.shape[1]
    for h in range(heads_kv):
        lanes = pl.ds(h * HEAD, HEAD)
        q = jnp.concatenate(
            [q_ref[:, pl.ds((h * group + g) * HEAD, HEAD)] for g in range(group)], axis=0
        )
        k = k_ref[:, :, lanes].reshape(rows * cache, HEAD)
        v = v_ref[:, :, lanes].reshape(rows * cache, HEAD)
        score = lax.dot_general(q, k, (((1,), (1,)), ((), ())), preferred_element_type=jnp.float32)
        score = score * scale + (diag_ref[...] + col_ref[0])
        kn = kn_ref[:, lanes].astype(jnp.float32)
        kn = jnp.concatenate([kn] * group, axis=0)
        own = jnp.sum(q.astype(jnp.float32) * kn, axis=1, keepdims=True) * scale
        top = jnp.maximum(jnp.max(score, axis=1, keepdims=True), own)
        e = jnp.exp(score - top)
        e_own = jnp.exp(own - top)
        total = jnp.sum(e, axis=1, keepdims=True) + e_own
        ctx = jnp.dot(e.astype(jnp.bfloat16), v, preferred_element_type=jnp.float32) / total
        own_w = e_own.astype(jnp.bfloat16).astype(jnp.float32) / total
        for g in range(group):
            part = slice(g * rows, (g + 1) * rows)
            ctx_ref[:, pl.ds((h * group + g) * HEAD, HEAD)] = ctx[part]
            own_ref[:, pl.ds(h * group + g, 1)] = own_w[part]


def attend(queries, new_key, cache_keys, cache_values, lengths):
    rows, width = queries.shape
    cache = cache_keys.shape[1]
    heads_kv = new_key.shape[1] // HEAD
    group = width // new_key.shape[1]
    blocks = rows // BLOCK
    wide = BLOCK * cache
    valid = jnp.arange(cache, dtype=jnp.int32)[None, :] < lengths[:, None]
    col = jnp.where(valid, 0.0, OFF).astype(jnp.float32).reshape(blocks, 1, wide)
    diag = jnp.where(
        (jnp.arange(group * BLOCK, dtype=jnp.int32) % BLOCK)[:, None]
        == (jnp.arange(wide, dtype=jnp.int32) // cache)[None, :],
        0.0,
        OFF,
    ).astype(jnp.float32)
    return pl.pallas_call(
        functools.partial(attend_kernel, heads_kv, group, 1.0 / math.sqrt(HEAD)),
        grid=(blocks,),
        in_specs=[
            pl.BlockSpec((BLOCK, width), lambda i: (i, 0)),
            pl.BlockSpec((BLOCK, new_key.shape[1]), lambda i: (i, 0)),
            pl.BlockSpec((BLOCK, cache, new_key.shape[1]), lambda i: (i, 0, 0)),
            pl.BlockSpec((BLOCK, cache, new_key.shape[1]), lambda i: (i, 0, 0)),
            pl.BlockSpec((1, 1, wide), lambda i: (i, 0, 0)),
            pl.BlockSpec((group * BLOCK, wide), lambda i: (0, 0)),
        ],
        out_specs=[
            pl.BlockSpec((BLOCK, width), lambda i: (i, 0)),
            pl.BlockSpec((BLOCK, heads_kv * group), lambda i: (i, 0)),
        ],
        out_shape=[
            jax.ShapeDtypeStruct((rows, width), jnp.float32),
            jax.ShapeDtypeStruct((rows, heads_kv * group), jnp.float32),
        ],
        compiler_params=pltpu.CompilerParams(vmem_limit_bytes=24 * 1024 * 1024),
        cost_estimate=pl.CostEstimate(
            flops=4 * rows * group * heads_kv * wide * HEAD,
            bytes_accessed=2 * 2 * cache_keys.size + 6 * queries.size,
            transcendentals=rows * group * heads_kv * wide,
        ),
        name="attend_cache",
    )(queries, new_key, cache_keys, cache_values, col, diag)


def finish_kernel(order, most, group, low_ref, mask_ref, b_ref, place_ref, base_ref, ctx_ref, own_ref, nv_ref, att_ref, delta):
    @pl.when(pl.program_id(0) == 0)
    def _():
        per = low_ref.shape[2] // most
        for i, o in enumerate(order):
            at = pl.ds((i % per) * most, most)
            low = low_ref[i // per, 0, at, :]
            for t in range(1, low_ref.shape[1]):
                low = low + low_ref[i // per, t, at, :]
            low = (low * mask_ref[pl.ds(o, 1), :]).astype(jnp.bfloat16)
            out = jnp.dot(low, b_ref[o], preferred_element_type=jnp.float32)
            delta[pl.ds(i * most, most), :] = out.astype(jnp.bfloat16).astype(jnp.float32)

    rows = jnp.dot(place_ref[...], delta[...].astype(jnp.bfloat16), preferred_element_type=jnp.float32)
    value = (base_ref[...] + rows).astype(jnp.bfloat16)
    nv_ref[...] = value
    value = value.astype(jnp.float32)
    for i in range(own_ref.shape[1]):
        lanes = pl.ds(i * HEAD, HEAD)
        h = i // group
        att_ref[:, lanes] = (
            ctx_ref[:, lanes] + own_ref[:, pl.ds(i, 1)] * value[:, h * HEAD : (h + 1) * HEAD]
        ).astype(jnp.bfloat16)


def finish(order, most, low, mask, b_all, place, base, ctx, own):
    rows, width = ctx.shape
    cols = base.shape[1]
    step = rows // 4
    whole = lambda a: pl.BlockSpec(a.shape, lambda i: (0,) * a.ndim)
    split = lambda a: pl.BlockSpec((step, a.shape[1]), lambda i: (i, 0))
    return pl.pallas_call(
        functools.partial(finish_kernel, order, most, width // cols),
        grid=(4,),
        in_specs=[whole(low), whole(mask), whole(b_all), split(place), split(base), split(ctx), split(own)],
        out_specs=[split(base), split(ctx)],
        out_shape=[
            jax.ShapeDtypeStruct((rows, cols), jnp.bfloat16),
            jax.ShapeDtypeStruct((rows, width), jnp.bfloat16),
        ],
        scratch_shapes=[pltpu.VMEM((place.shape[1], cols), jnp.float32)],
        compiler_params=pltpu.CompilerParams(vmem_limit_bytes=40 * 1024 * 1024),
        cost_estimate=pl.CostEstimate(
            flops=4 * rows * place.shape[1] * cols, bytes_accessed=6 * rows * width, transcendentals=0
        ),
        name="finish_rows",
    )(low, mask, b_all, place, base, ctx, own)


def body(
    normed_rows,
    value_weight,
    adapter_a,
    adapter_b,
    page_table,
    group_list,
    seg_len,
    kv_len,
    queries,
    new_key,
    cache_keys,
    cache_values,
):
    tp_index = lax.axis_index("tp")
    tps = lax.axis_size("tp")
    lines, columns = lax.axis_size("line"), lax.axis_size("slab")
    groups = lines * columns
    me = lax.axis_index("line") * columns + lax.axis_index("slab")
    rows_count = normed_rows.shape[0]
    part = normed_rows.shape[1] // tps
    per_owner, _, rank = adapter_a.shape
    adapters_count = page_table.shape[0]
    lens = seg_len[0]
    slots = lens.shape[0]
    most = 2 * rows_count // slots

    down = adapter_a.transpose(0, 2, 1).reshape(per_owner * rank, part)
    down = lax.all_gather(down, "line")
    up = lax.all_gather(adapter_b.reshape(per_owner * rank, -1), ("line", "slab"))

    ends = jnp.cumsum(lens)
    starts = ends - lens
    rowpos = jnp.arange(rows_count, dtype=jnp.int32)
    in_segment = (rowpos[:, None] >= starts[None, :]) & (rowpos[:, None] < ends[None, :])
    listed = lax.dynamic_index_in_dim(group_list, me, 0, keepdims=False)
    positions = jnp.sum(
        jnp.where(
            listed[:, None] == jnp.arange(adapters_count, dtype=jnp.int32)[None, :],
            page_table[None, :],
            0,
        ),
        axis=1,
    )
    owners = positions // per_owner
    local = positions % per_owner
    place_of = ((owners % columns) * lines + owners // columns) * most - starts
    target = rowpos + jnp.sum(jnp.where(in_segment, place_of[None, :], 0), axis=1)
    spots = jnp.arange(groups * most, dtype=jnp.int32)
    placing = (spots[:, None] == target[None, :]).astype(jnp.bfloat16)
    taking = (target[:, None] == spots[None, :]).astype(jnp.bfloat16)
    owner_hit = jnp.arange(groups, dtype=jnp.int32)[:, None] == owners[None, :]
    which = jnp.sum(jnp.where(owner_hit, local[None, :], 0), axis=1)
    mask = (
        which[:, None] == (jnp.arange(per_owner * rank, dtype=jnp.int32) // rank)[None, :]
    ).astype(jnp.float32)

    x_part = lax.dynamic_slice_in_dim(normed_rows, tp_index * part, part, 1)
    placed = jnp.dot(placing, x_part, preferred_element_type=jnp.float32).astype(jnp.bfloat16)
    arrived = lax.all_to_all(
        placed.reshape(columns, lines * most, part), "slab", split_axis=0, concat_axis=0, tiled=True
    )
    base = jnp.dot(normed_rows, value_weight, preferred_element_type=jnp.float32)
    ctx, own = attend(queries, new_key, cache_keys, cache_values, kv_len[0])

    low = jnp.stack(
        [
            jnp.einsum(
                "smd,nd->smn",
                arrived[:, z * most : (z + 1) * most],
                down[z],
                preferred_element_type=jnp.float32,
            )
            for z in range(lines)
        ],
        axis=1,
    ).reshape(columns, 1, lines * most, per_owner * rank)
    low = jnp.broadcast_to(low, (columns, tps) + low.shape[2:])
    low = lax.all_to_all(
        low.reshape((columns * tps,) + low.shape[2:]),
        ("slab", "tp"),
        split_axis=0,
        concat_axis=0,
        tiled=True,
    ).reshape(low.shape)
    order = [z * columns + s for s in range(columns) for z in range(lines)]
    return tuple(finish(order, most, low, mask, up, taking, base, ctx, own))


def solution(mesh):
    rows, tps = mesh.shape["rows"], mesh.shape["tp"]
    slab = 2 * math.isqrt(rows // 4)
    split = Mesh(mesh.devices.reshape(rows // slab, slab, tps), ("line", "slab", "tp"))
    pair = ("line", "slab")
    return jax.shard_map(
        body,
        mesh=split,
        in_specs=(
            P(pair, None),
            P(None, "tp"),
            P(pair, "tp", None),
            P(pair, None, "tp"),
            P(),
            P(),
            P(pair, None),
            P(pair, None),
            P(pair, "tp"),
            P(pair, "tp"),
            P(pair, None, "tp"),
            P(pair, None, "tp"),
        ),
        out_specs=(P(pair, "tp"), P(pair, "tp")),
        check_vma=False,
    )
```

time: 184 us -> 150 us (0.82)
  local copies, waits for them, and re-layouts: 63.6 us -> 15 us
  waiting for transfers between devices: 34.9 us -> 67.3 us
  Pallas kernels: 0 us -> 22.9 us
  starting transfers between devices: 26.2 us -> 8.75 us
  matrix products: 34.2 us -> 18 us
  between operations: 0.81 us -> 14.2 us
  blocking collectives: 13.1 us -> 0 us
  other arithmetic: 9.33 us -> 2.89 us
    all_gather x0 -> x2, waiting for transfers between devices: none -> 53.6 us  [the longest x1 29.8 us: body(): lax.all_gather(adapter_b.reshape(per_owner * rank, -1), ('line', 'slab'))]
    reshape x4 -> x1, local copies, waits for them, and re-layouts: 30.3 us -> 0.73 us  [the longest x1 14.8 us: body(): k_four = cache_keys.reshape(rows_count, -1, heads_kv, HEAD)]
    pallas_call x0 -> x2, Pallas kernels: none -> 22.9 us  [the longest x1 19.6 us: attend(): pl.pallas_call(functools.partial(attend_kernel, heads_kv, group, 1.0 / ma...]
    all_to_all x2, waiting for transfers between devices: 34.9 us -> 12.3 us  [the longest x1 12.3 us: body(): lax.all_to_all(placed.reshape(columns, lines * most, part), 'slab', split...]
    unnamed x19 -> x23, local copies, waits for them, and re-layouts: 31.7 us -> 13.1 us
    all_to_all x2, starting transfers between devices: 26.2 us -> 8.67 us  [the longest x1 4.97 us: body(): lax.all_to_all(placed.reshape(columns, lines * most, part), 'slab', split...]
    dot_general x5 -> x4, matrix products: 22.4 us -> 7.47 us  [body(): jnp.einsum('smd,nd->smn', arrived[:, z * most:(z + 1) * most], down[z], p...]
    psum x1 -> x0, blocking collectives: 13.1 us -> none  [body(): low = lax.psum(low_part, 'tp').astype(jnp.bfloat16)]
  transfers between devices with their start and end apart: 2 -> 4, of which waited for: 1 -> 3; matrix products, arithmetic and copies ran while one was open for 47% -> 16% of each run, Pallas kernels for 0% -> 13%
where the time goes in v1:
time: 150 us; the launch traced here: 149 us
  waiting for transfers between devices  67.3 us (45%)
  Pallas kernels  22.9 us (15%)
  matrix products  18 us (12%)
  local copies, waits for them, and re-layouts  15 us (10%)
  between operations  14.2 us (9%)
  starting transfers between devices  8.75 us (6%)
  other arithmetic  2.89 us (2%)
    all_gather x1, waiting for transfers between devices, body(): lax.all_gather(adapter_b.reshape(per_owner * rank, -1), ('line', 'slab'))  29.8 us
    all_gather x1, waiting for transfers between devices, body(): down = lax.all_gather(down, 'line')  23.8 us
    pallas_call x1, Pallas kernels, attend(): pl.pallas_call(functools.partial(attend_kernel, heads_kv, group, 1.0 / ma...  19.6 us
    unnamed x23, local copies, waits for them, and re-layouts  13.1 us
    all_to_all x1, waiting for transfers between devices, body(): lax.all_to_all(placed.reshape(columns, lines * most, part), 'slab', split...  12.3 us
    dot_general x4, matrix products, body(): jnp.einsum('smd,nd->smn', arrived[:, z * most:(z + 1) * most], down[z], p...  7.47 us
    dot_general x1, matrix products, body(): jnp.dot(normed_rows, value_weight, preferred_element_type=jnp.float32)  5.69 us
    all_to_all x1, starting transfers between devices, body(): lax.all_to_all(placed.reshape(columns, lines * most, part), 'slab', split...  4.97 us
  transfers between devices with their start and end apart: 4, of which 3 were waited for; matrix products, arithmetic and copies ran while one was open for 16% of the time, Pallas kernels for 13%

profile of v1, /device:TPU:0, one launch (start us, length us, event | category | flops | bytes accessed | tf_op | source)
XLA Modules:
  0.0 149.1 jit_solution(7458101259843267881)
XLA Ops:
  7.2 0.0 copy-start
  7.2 0.0 all-gather.3.cloned.1.call-start
  7.2 0.7 all-gather.3.cloned.1.call-update
  7.9 0.7 copy.19
  8.7 0.1 reduce
  8.8 0.0 copy-done
  8.8 0.8 select_reduce_fusion.2
  9.7 0.7 fusion.14
  10.4 0.1 select_reduce_fusion
  10.4 4.8 %convolution_convert_fusion = bf16[512,4096]{1,0:T(8,128)(2,1)} fusion(bf16[256,8192]{1,0:T(8,128)(2,1)} %param.12, s32[]{:T(128)S(6)} %select_n.117, s32[256]{0:T(256)S(1)} %iota_add_fusion), kind=kOutput, calls=%fused_computation | convolution fusion | flops 1075970048 | bytes 6292484 | tf_op jit(solution)/shard_map/dot_general | solution.py:194
  15.3 0.0 copy-start.9
  15.3 0.0 copy-start.5
  15.3 0.0 copy-start.7
  15.3 5.0 %all-to-all-start = ((bf16[4,128,4096]{2,1,0:T(8,128)(2,1)}), bf16[4,128,4096]{2,1,0:T(8,128)(2,1)}, u32[]{:S(2)}, u32[]{:S(2)}) async-start(bf16[4,128,4096]{2,1,0:T(8,128)(2,1)} %bitcast.58), calls=%async_computation | async-start | bytes 8388608 | tf_op jit(solution)/shard_map/all_to_all | solution.py:195
  20.3 0.0 all-gather.5.cloned.1.call-start
  20.3 0.7 all-gather.5.cloned.1.call-update
  21.0 0.5 broadcast.326
  21.5 0.0 copy-done.9
  21.5 0.7 reduce.5
  22.2 0.1 lt.74
  22.3 0.1 lt.75
  22.4 0.1 lt.76
  22.5 0.1 lt.72
  22.6 0.1 select_reduce_fusion.1
  22.8 0.1 compare_select_fusion.diag_ref
  22.9 0.0 copy-done.5
  22.9 0.0 copy-done.7
  22.9 0.0 copy-start.1
  22.9 3.4 %copy-done.1 = bf16[256,32,512]{2,1,0:T(8,128)(2,1)S(1)} copy-done((bf16[256,32,512]{2,1,0:T(8,128)(2,1)S(1)}, bf16[256,32,512]{2,1,0:T(8,128)(2,1)}, u32[]{:S(2)}) %copy-start.1) | copy-done | bytes 8388632
  26.3 0.0 copy-start.2
  26.3 3.4 %copy-done.2 = bf16[256,32,512]{2,1,0:T(8,128)(2,1)S(1)} copy-done((bf16[256,32,512]{2,1,0:T(8,128)(2,1)S(1)}, bf16[256,32,512]{2,1,0:T(8,128)(2,1)}, u32[]{:S(2)}) %copy-start.2) | copy-done | bytes 8388632
  29.7 0.0 copy-start.8
  29.7 19.6 %attend_cache.1 = (f32[256,4096]{1,0:T(8,128)S(1)}, f32[256,32]{1,0:T(8,128)S(1)}) custom-call(bf16[256,4096]{1,0:T(8,128)(2,1)S(1)} %copy-done.5, bf16[256,512]{1,0:T(8,128)(2,1)S(1)} %copy-done.7, bf16[256,32,512]{2,1,0:T(8,128)(2,1)S(1)} %copy-done.1, bf16[256,32,512]{2,1,0:T(8,128)(2,1)S(1)} %copy-done.2, ...), custom_call_target="tpu_custom_call" | custom-call | flops 2147483648 | bytes 23068672 | tf_op jit(solution)/shard_map/attend_cache/pallas_call | solution.py:58
  49.3 0.0 copy-start.3
  49.3 1.9 %copy-done.3 = f32[256,4096]{1,0:T(8,128)} copy-done((f32[256,4096]{1,0:T(8,128)}, f32[256,4096]{1,0:T(8,128)S(1)}, u32[]{:S(2)}) %copy-start.3) | copy-done | bytes 4194328
  51.2 0.0 copy-done.8
  51.2 5.7 %fusion.15.base_ref = f32[256,512]{1,0:T(8,128)S(1)} fusion(bf16[256,8192]{1,0:T(8,128)(2,1)S(1)} %copy-done.8, bf16[8192,512]{1,0:T(8,128)(2,1)} %param.13), kind=kOutput, calls=%fused_computation.65 | convolution fusion | flops 2147483648 | bytes 13107200 | tf_op jit(solution)/shard_map/dot_general | solution.py:198
  56.9 12.3 %all-to-all-done = bf16[4,128,4096]{2,1,0:T(8,128)(2,1)} async-done(((bf16[4,128,4096]{2,1,0:T(8,128)(2,1)}), bf16[4,128,4096]{2,1,0:T(8,128)(2,1)}, u32[]{:S(2)}, u32[]{:S(2)}) %all-to-all-start) | async-done | bytes 4194336 | tf_op jit(solution)/shard_map/all_to_all | solution.py:195
  69.3 23.8 %all-gather.3.cloned.1.call-done = bf16[4,128,4096]{2,1,0:T(8,128)(2,1)} async-done(((bf16[1,128,4096]{2,1,0:T(8,128)(2,1)}), bf16[4,128,4096]{2,1,0:T(8,128)(2,1)}) %all-gather.3.cloned.1.call-update) | async-done | bytes 4194320 | tf_op jit(solution)/shard_map/all_gather | solution.py:164
  93.1 0.0 copy-start.10
  93.1 2.1 %convolution_bitcast_fusion.1 = f32[4,1,32,128]{3,2,0,1:T(8,128)S(1)} fusion(bf16[4,128,4096]{2,1,0:T(8,128)(2,1)} %all-gather.3.cloned.1.call-done, bf16[4,128,4096]{2,1,0:T(8,128)(2,1)} %all-to-all-done), kind=kOutput, calls=%fused_computation.3 | convolution fusion | flops 134217728 | bytes 2162688 | tf_op jit(solution)/shard_map/smd,nd->smn/dot_general | solution.py:203
  95.2 2.0 %convolution_bitcast_fusion.2 = f32[4,1,32,128]{3,2,0,1:T(8,128)S(1)} fusion(bf16[4,128,4096]{2,1,0:T(8,128)(2,1)} %all-gather.3.cloned.1.call-done, bf16[4,128,4096]{2,1,0:T(8,128)(2,1)} %all-to-all-done), kind=kOutput, calls=%fused_computation.4 | convolution fusion | flops 134217728 | bytes 2162688 | tf_op jit(solution)/shard_map/smd,nd->smn/dot_general | solution.py:203
  97.2 0.0 copy-done.10
  97.2 1.7 %convolution_bitcast_fusion.3 = f32[4,1,32,128]{3,2,0,1:T(8,128)S(1)} fusion(bf16[4,128,4096]{2,1,0:T(8,128)(2,1)S(1)} %copy-done.10, bf16[4,128,4096]{2,1,0:T(8,128)(2,1)} %all-to-all-done), kind=kOutput, calls=%fused_computation.5 | convolution fusion | flops 134217728 | bytes 2162688 | tf_op jit(solution)/shard_map/smd,nd->smn/dot_general | solution.py:203
  98.9 1.7 %convolution_bitcast_fusion = f32[4,1,32,128]{3,2,0,1:T(8,128)S(1)} fusion(bf16[4,128,4096]{2,1,0:T(8,128)(2,1)S(1)} %copy-done.10, bf16[4,128,4096]{2,1,0:T(8,128)(2,1)} %all-to-all-done), kind=kOutput, calls=%fused_computation.2 | convolution fusion | flops 134217728 | bytes 2162688 | tf_op jit(solution)/shard_map/smd,nd->smn/dot_general | solution.py:203
  100.6 0.8 broadcast_in_dim.87
  101.5 3.7 %all-to-all-start.1 = ((f32[8,128,128]{2,1,0:T(8,128)}), f32[8,128,128]{2,1,0:T(8,128)S(1)}, u32[]{:S(2)}, u32[]{:S(2)}) async-start(f32[8,128,128]{2,1,0:T(8,128)} %bitcast.21), calls=%async_computation.1 | async-start | bytes 1048576 | tf_op jit(solution)/shard_map/all_to_all | solution.py:214
  105.2 0.1 compare_convert_fusion.mask_ref
  105.2 0.1 fusion.5.place_ref
  105.4 29.8 %all-gather.5.cloned.1.call-done.b_ref = bf16[16,128,512]{2,1,0:T(8,128)(2,1)} async-done(((bf16[1,128,512]{2,1,0:T(8,128)(2,1)}), bf16[16,128,512]{2,1,0:T(8,128)(2,1)}) %all-gather.5.cloned.1.call-update) | async-done | bytes 2097168 | tf_op jit(solution)/shard_map/all_gather | solution.py:165
  135.1 0.0 all-to-all-done.1
  135.1 0.0 copy-start.4
  135.1 2.2 %copy-done.4 = f32[256,4096]{1,0:T(8,128)S(1)} copy-done((f32[256,4096]{1,0:T(8,128)S(1)}, f32[256,4096]{1,0:T(8,128)}, u32[]{:S(2)}) %copy-start.4) | copy-done | bytes 4194328
  137.3 0.0 copy-start.6
  137.3 1.6 %copy-done.6 = bf16[16,128,512]{2,1,0:T(8,128)(2,1)S(1)} copy-done((bf16[16,128,512]{2,1,0:T(8,128)(2,1)S(1)}, bf16[16,128,512]{2,1,0:T(8,128)(2,1)}, u32[]{:S(2)}) %copy-start.6) | copy-done | bytes 2097176
  138.9 3.3 %finish_rows.1 = (bf16[256,512]{1,0:T(8,128)(2,1)}, bf16[256,4096]{1,0:T(8,128)(2,1)}) custom-call(f32[4,2,128,128]{3,2,1,0:T(8,128)S(1)} %bitcast.57, f32[16,128]{1,0:T(8,128)S(1)} %compare_convert_fusion.mask_ref, bf16[16,128,512]{2,1,0:T(8,128)(2,1)S(1)} %copy-done.6, bf16[256,512]{1,0:T(8,128)(2,1)S(1)} %fusion.5.place_ref, ...), custom_call_target="tpu_custom_call" | custom-call | flops 268435456 | bytes 6291456 | tf_op jit(solution)/shard_map/finish_rows/pallas_call | solution.py:118
  (11 shorter events, 0.1 us)
Async XLA Ops:
  7.2 1.6 %copy-start = (s32[16,16]{1,0:T(8,128)S(1)}, s32[16,16]{1,0:T(8,128)}, u32[]{:S(2)}) copy-start(s32[16,16]{1,0:T(8,128)} %param.17) | copy-start | bytes 3076
  7.2 85.9 %all-gather.3.cloned.1.call-start = ((), (), s32[]{:S(2)}) async-start(), calls=%async_computation.2 | async-start | bytes 5242880 | tf_op jit(solution)/shard_map/all_gather | solution.py:164
  15.3 6.3 %copy-start.9 = (s32[1,256]{1,0:T(1,128)S(1)}, s32[1,256]{1,0:T(1,128)}, u32[]{:S(2)}) copy-start(s32[1,256]{1,0:T(1,128)} %param.19) | copy-start | bytes 3076
  15.3 7.6 %copy-start.5 = (bf16[256,4096]{1,0:T(8,128)(2,1)S(1)}, bf16[256,4096]{1,0:T(8,128)(2,1)}, u32[]{:S(2)}) copy-start(bf16[256,4096]{1,0:T(8,128)(2,1)} %q_ref.1) | copy-start | bytes 6291460
  15.3 7.6 %copy-start.7 = (bf16[256,512]{1,0:T(8,128)(2,1)S(1)}, bf16[256,512]{1,0:T(8,128)(2,1)}, u32[]{:S(2)}) copy-start(bf16[256,512]{1,0:T(8,128)(2,1)} %kn_ref.1) | copy-start | bytes 786436
  15.3 54.0 %all-to-all-start = ((bf16[4,128,4096]{2,1,0:T(8,128)(2,1)}), bf16[4,128,4096]{2,1,0:T(8,128)(2,1)}, u32[]{:S(2)}, u32[]{:S(2)}) async-start(bf16[4,128,4096]{2,1,0:T(8,128)(2,1)} %bitcast.58), calls=%async_computation | async-start | bytes 8388608 | tf_op jit(solution)/shard_map/all_to_all | solution.py:195
  20.3 114.9 %all-gather.5.cloned.1.call-start = ((), (), s32[]{:S(2)}) async-start(), calls=%async_computation.3 | async-start | bytes 2228224 | tf_op jit(solution)/shard_map/all_gather | solution.py:165
  22.9 3.4 %copy-start.1 = (bf16[256,32,512]{2,1,0:T(8,128)(2,1)S(1)}, bf16[256,32,512]{2,1,0:T(8,128)(2,1)}, u32[]{:S(2)}) copy-start(bf16[256,32,512]{2,1,0:T(8,128)(2,1)} %k_ref.1) | copy-start | bytes 25165828
  26.3 3.4 %copy-start.2 = (bf16[256,32,512]{2,1,0:T(8,128)(2,1)S(1)}, bf16[256,32,512]{2,1,0:T(8,128)(2,1)}, u32[]{:S(2)}) copy-start(bf16[256,32,512]{2,1,0:T(8,128)(2,1)} %v_ref.1) | copy-start | bytes 25165828
  29.7 21.5 %copy-start.8 = (bf16[256,8192]{1,0:T(8,128)(2,1)S(1)}, bf16[256,8192]{1,0:T(8,128)(2,1)}, u32[]{:S(2)}) copy-start(bf16[256,8192]{1,0:T(8,128)(2,1)} %param.12) | copy-start | bytes 12582916
  49.3 1.9 %copy-start.3 = (f32[256,4096]{1,0:T(8,128)}, f32[256,4096]{1,0:T(8,128)S(1)}, u32[]{:S(2)}) copy-start(f32[256,4096]{1,0:T(8,128)S(1)} %get-tuple-element.4.ctx_ref) | copy-start | bytes 12582916
  93.1 4.1 %copy-start.10 = (bf16[4,128,4096]{2,1,0:T(8,128)(2,1)S(1)}, bf16[4,128,4096]{2,1,0:T(8,128)(2,1)}, u32[]{:S(2)}) copy-start(bf16[4,128,4096]{2,1,0:T(8,128)(2,1)} %all-gather.3.cloned.1.call-done) | copy-start | bytes 12582916
  101.5 33.7 %all-to-all-start.1 = ((f32[8,128,128]{2,1,0:T(8,128)}), f32[8,128,128]{2,1,0:T(8,128)S(1)}, u32[]{:S(2)}, u32[]{:S(2)}) async-start(f32[8,128,128]{2,1,0:T(8,128)} %bitcast.21), calls=%async_computation.1 | async-start | bytes 1048576 | tf_op jit(solution)/shard_map/all_to_all | solution.py:214
  135.1 2.2 %copy-start.4 = (f32[256,4096]{1,0:T(8,128)S(1)}, f32[256,4096]{1,0:T(8,128)}, u32[]{:S(2)}) copy-start(f32[256,4096]{1,0:T(8,128)} %copy-done.3) | copy-start | bytes 12582916
  137.3 1.6 %copy-start.6 = (bf16[16,128,512]{2,1,0:T(8,128)(2,1)S(1)}, bf16[16,128,512]{2,1,0:T(8,128)(2,1)}, u32[]{:S(2)}) copy-start(bf16[16,128,512]{2,1,0:T(8,128)(2,1)} %all-gather.5.cloned.1.call-done.b_ref) | copy-start | bytes 6291460
Sparse Core Ops, SparseCore 0:
  9.6 83.4 all-gather.2
  95.2 39.8 all-gather.4

commit v2 on v1

--- a/solution.py
+++ b/solution.py
@@ -84,20 +84,8 @@
     )(queries, new_key, cache_keys, cache_values, col, diag)
 
 
-def finish_kernel(order, most, group, low_ref, mask_ref, b_ref, place_ref, base_ref, ctx_ref, own_ref, nv_ref, att_ref, delta):
-    @pl.when(pl.program_id(0) == 0)
-    def _():
-        per = low_ref.shape[2] // most
-        for i, o in enumerate(order):
-            at = pl.ds((i % per) * most, most)
-            low = low_ref[i // per, 0, at, :]
-            for t in range(1, low_ref.shape[1]):
-                low = low + low_ref[i // per, t, at, :]
-            low = (low * mask_ref[pl.ds(o, 1), :]).astype(jnp.bfloat16)
-            out = jnp.dot(low, b_ref[o], preferred_element_type=jnp.float32)
-            delta[pl.ds(i * most, most), :] = out.astype(jnp.bfloat16).astype(jnp.float32)
-
-    rows = jnp.dot(place_ref[...], delta[...].astype(jnp.bfloat16), preferred_element_type=jnp.float32)
+def finish_kernel(group, delta_ref, place_ref, base_ref, ctx_ref, own_ref, nv_ref, att_ref):
+    rows = jnp.dot(place_ref[...], delta_ref[...], preferred_element_type=jnp.float32)
     value = (base_ref[...] + rows).astype(jnp.bfloat16)
     nv_ref[...] = value
     value = value.astype(jnp.float32)
@@ -109,28 +97,32 @@
         ).astype(jnp.bfloat16)
 
 
-def finish(order, most, low, mask, b_all, place, base, ctx, own):
+def finish(delta, place, base, ctx, own):
     rows, width = ctx.shape
     cols = base.shape[1]
     step = rows // 4
-    whole = lambda a: pl.BlockSpec(a.shape, lambda i: (0,) * a.ndim)
     split = lambda a: pl.BlockSpec((step, a.shape[1]), lambda i: (i, 0))
     return pl.pallas_call(
-        functools.partial(finish_kernel, order, most, width // cols),
+        functools.partial(finish_kernel, width // cols),
         grid=(4,),
-        in_specs=[whole(low), whole(mask), whole(b_all), split(place), split(base), split(ctx), split(own)],
+        in_specs=[
+            pl.BlockSpec(delta.shape, lambda i: (0, 0)),
+            split(place),
+            split(base),
+            split(ctx),
+            split(own),
+        ],
         out_specs=[split(base), split(ctx)],
         out_shape=[
             jax.ShapeDtypeStruct((rows, cols), jnp.bfloat16),
             jax.ShapeDtypeStruct((rows, width), jnp.bfloat16),
         ],
-        scratch_shapes=[pltpu.VMEM((place.shape[1], cols), jnp.float32)],
-        compiler_params=pltpu.CompilerParams(vmem_limit_bytes=40 * 1024 * 1024),
+        compiler_params=pltpu.CompilerParams(vmem_limit_bytes=32 * 1024 * 1024),
         cost_estimate=pl.CostEstimate(
             flops=4 * rows * place.shape[1] * cols, bytes_accessed=6 * rows * width, transcendentals=0
         ),
         name="finish_rows",
-    )(low, mask, b_all, place, base, ctx, own)
+    )(delta, place, base, ctx, own)
 
 
 def body(
@@ -161,33 +153,36 @@
     most = 2 * rows_count // slots
 
     down = adapter_a.transpose(0, 2, 1).reshape(per_owner * rank, part)
-    down = lax.all_gather(down, "line")
-    up = lax.all_gather(adapter_b.reshape(per_owner * rank, -1), ("line", "slab"))
+    maps = jnp.concatenate([down, adapter_b.reshape(per_owner * rank, -1)], axis=1)
+    maps = lax.all_gather(maps, "line")
 
     ends = jnp.cumsum(lens)
     starts = ends - lens
     rowpos = jnp.arange(rows_count, dtype=jnp.int32)
     in_segment = (rowpos[:, None] >= starts[None, :]) & (rowpos[:, None] < ends[None, :])
-    listed = lax.dynamic_index_in_dim(group_list, me, 0, keepdims=False)
     positions = jnp.sum(
         jnp.where(
-            listed[:, None] == jnp.arange(adapters_count, dtype=jnp.int32)[None, :],
-            page_table[None, :],
+            group_list[:, :, None] == jnp.arange(adapters_count, dtype=jnp.int32),
+            page_table,
             0,
         ),
-        axis=1,
-    )
-    owners = positions // per_owner
+        axis=2,
+    )
+    held = positions // per_owner
     local = positions % per_owner
+    owners = lax.dynamic_index_in_dim(held, me, 0, keepdims=False)
     place_of = ((owners % columns) * lines + owners // columns) * most - starts
     target = rowpos + jnp.sum(jnp.where(in_segment, place_of[None, :], 0), axis=1)
     spots = jnp.arange(groups * most, dtype=jnp.int32)
     placing = (spots[:, None] == target[None, :]).astype(jnp.bfloat16)
     taking = (target[:, None] == spots[None, :]).astype(jnp.bfloat16)
-    owner_hit = jnp.arange(groups, dtype=jnp.int32)[:, None] == owners[None, :]
-    which = jnp.sum(jnp.where(owner_hit, local[None, :], 0), axis=1)
-    mask = (
-        which[:, None] == (jnp.arange(per_owner * rank, dtype=jnp.int32) // rank)[None, :]
+    hit = held[:, None, :] == jnp.arange(groups, dtype=jnp.int32)[None, :, None]
+    which = jnp.sum(jnp.where(hit, local[:, None, :], 0), axis=2)
+    which = which.reshape(lines, columns, lines, columns)
+    which = lax.dynamic_index_in_dim(which, lax.axis_index("line"), 0, keepdims=False)
+    which = lax.dynamic_index_in_dim(which, lax.axis_index("slab"), 2, keepdims=False)
+    chosen = (
+        which[:, :, None, None] == (jnp.arange(per_owner * rank, dtype=jnp.int32) // rank)
     ).astype(jnp.float32)
 
     x_part = lax.dynamic_slice_in_dim(normed_rows, tp_index * part, part, 1)
@@ -203,23 +198,28 @@
             jnp.einsum(
                 "smd,nd->smn",
                 arrived[:, z * most : (z + 1) * most],
-                down[z],
+                maps[z, :, :part],
                 preferred_element_type=jnp.float32,
             )
             for z in range(lines)
         ],
         axis=1,
-    ).reshape(columns, 1, lines * most, per_owner * rank)
-    low = jnp.broadcast_to(low, (columns, tps) + low.shape[2:])
-    low = lax.all_to_all(
-        low.reshape((columns * tps,) + low.shape[2:]),
-        ("slab", "tp"),
-        split_axis=0,
-        concat_axis=0,
-        tiled=True,
-    ).reshape(low.shape)
-    order = [z * columns + s for s in range(columns) for z in range(lines)]
-    return tuple(finish(order, most, low, mask, up, taking, base, ctx, own))
+    )
+    total = low
+    for hop in range(1, tps):
+        total = total + lax.ppermute(low, "tp", [(t, (t + hop) % tps) for t in range(tps)])
+    total = (total * chosen).astype(jnp.bfloat16)
+    delta = jnp.stack(
+        [
+            jnp.einsum(
+                "smn,nc->smc", total[:, z], maps[z, :, part:], preferred_element_type=jnp.float32
+            ).astype(jnp.bfloat16)
+            for z in range(lines)
+        ],
+        axis=1,
+    ).reshape(columns, lines * most, -1)
+    delta = lax.all_to_all(delta, "slab", split_axis=0, concat_axis=0, tiled=True)
+    return tuple(finish(delta.reshape(groups * most, -1), taking, base, ctx, own))
 
 
 def solution(mesh):

time: 150 us -> 167 us (1.11)
  waiting for transfers between devices: 67.3 us -> 77 us
  other arithmetic: 2.89 us -> 5.95 us
  matrix products: 18 us -> 20.1 us
    all_to_all x1, waiting for transfers between devices: 12.3 us -> 39.6 us  [body(): lax.all_to_all(placed.reshape(columns, lines * most, part), 'slab', split...]
    all_gather x2 -> x1, waiting for transfers between devices: 53.6 us -> 30.9 us  [body(): maps = lax.all_gather(maps, 'line')]
    ppermute x0 -> x1, waiting for transfers between devices: none -> 6.52 us  [body(): lax.ppermute(low, 'tp', [(t, (t + hop) % tps) for t in range(tps)])]
    concatenate x0 -> x1, other arithmetic: none -> 2.4 us  [body(): jnp.concatenate([down, adapter_b.reshape(per_owner * rank, -1)], axis=1)]
    unnamed x23 -> x21, local copies, waits for them, and re-layouts: 13.1 us -> 13.9 us
    dot_general x4 -> x8, matrix products: 7.47 us -> 8.25 us  [the longest x4 7.58 us: body(): jnp.einsum('smd,nd->smn', arrived[:, z * most:(z + 1) * most], maps[z, :,...]
  transfers between devices with their start and end apart: 4 -> 4, of which waited for: 3 -> 3; matrix products, arithmetic and copies ran while one was open for 16% -> 10% of each run, Pallas kernels for 13% -> 12%
where the time goes in v2:
time: 167 us; the launch traced here: 166 us
  waiting for transfers between devices  77 us (46%)
  Pallas kernels  22.4 us (13%)
  matrix products  20.1 us (12%)
  local copies, waits for them, and re-layouts  16.1 us (10%)
  between operations  14.3 us (9%)
  starting transfers between devices  10.2 us (6%)
  other arithmetic  5.95 us (4%)
    all_to_all x1, waiting for transfers between devices, body(): lax.all_to_all(placed.reshape(columns, lines * most, part), 'slab', split...  39.6 us
    all_gather x1, waiting for transfers between devices, body(): maps = lax.all_gather(maps, 'line')  30.9 us
    pallas_call x1, Pallas kernels, attend(): pl.pallas_call(functools.partial(attend_kernel, heads_kv, group, 1.0 / ma...  19.6 us
    unnamed x21, local copies, waits for them, and re-layouts  13.9 us
    dot_general x4, matrix products, body(): jnp.einsum('smd,nd->smn', arrived[:, z * most:(z + 1) * most], maps[z, :,...  7.58 us
    dot_general x1, matrix products, body(): jnp.dot(normed_rows, value_weight, preferred_element_type=jnp.float32)  6.99 us
    ppermute x1, waiting for transfers between devices, body(): lax.ppermute(low, 'tp', [(t, (t + hop) % tps) for t in range(tps)])  6.52 us
    all_to_all x1, starting transfers between devices, body(): lax.all_to_all(placed.reshape(columns, lines * most, part), 'slab', split...  5.14 us
  transfers between devices with their start and end apart: 4, of which 3 were waited for; matrix products, arithmetic and copies ran while one was open for 10% of the time, Pallas kernels for 12%

profile of v2, /device:TPU:0, one launch (start us, length us, event | category | flops | bytes accessed | tf_op | source)
XLA Modules:
  0.0 166.1 jit_solution(17202176501829674906)
XLA Ops:
  7.2 0.0 all-gather.3.cloned.1.call-start
  7.2 2.4 %pad_maximum_fusion = bf16[128,4608]{1,0:T(8,128)(2,1)} fusion(bf16[128,512]{1,0:T(8,128)(2,1)} %bitcast.86, bf16[128,4096]{1,0:T(8,128)(2,1)} %bitcast.85), kind=kLoop, calls=%fused_computation.2 | loop fusion | flops 2359296 | bytes 2359296 | tf_op jit(solution)/shard_map/concatenate | solution.py:156
  9.6 0.0 all-gather.3.cloned.1.call-update
  9.6 0.7 copy.22
  10.4 0.1 reduce
  10.5 1.1 select_reduce_fusion.1
  11.7 0.7 fusion.20
  12.4 0.1 select_reduce_fusion.2
  12.5 4.9 %convolution_convert_fusion = bf16[512,4096]{1,0:T(8,128)(2,1)} fusion(bf16[256,8192]{1,0:T(8,128)(2,1)} %param.12, s32[]{:T(128)S(6)} %select_n.113, s32[256]{0:T(256)S(1)} %iota_add_fusion), kind=kOutput, calls=%fused_computation | convolution fusion | flops 1075970048 | bytes 6292484 | tf_op jit(solution)/shard_map/dot_general | solution.py:189
  17.3 0.0 copy-start.9
  17.3 5.1 %all-to-all-start = ((bf16[4,128,4096]{2,1,0:T(8,128)(2,1)}), bf16[4,128,4096]{2,1,0:T(8,128)(2,1)}, u32[]{:S(2)}, u32[]{:S(2)}) async-start(bf16[4,128,4096]{2,1,0:T(8,128)(2,1)} %bitcast.83), calls=%async_computation | async-start | bytes 8388608 | tf_op jit(solution)/shard_map/all_to_all | solution.py:190
  22.5 0.3 select_reduce_fusion
  22.8 0.1 reshape.172
  22.9 0.1 constant_dynamic-slice_fusion
  23.0 0.1 copy.25
  23.1 0.5 broadcast.223
  23.6 0.0 copy-done.9
  23.6 0.7 reduce.5
  24.3 0.1 lt.86
  24.4 0.1 lt.87
  24.5 0.1 lt.88
  24.6 0.1 lt.84
  24.7 0.1 compare_convert_fusion
  24.8 7.0 %fusion.21.base_ref = f32[256,512]{1,0:T(8,128)S(1)} fusion(bf16[256,8192]{1,0:T(8,128)(2,1)} %param.12, bf16[8192,512]{1,0:T(8,128)(2,1)} %param.13), kind=kOutput, calls=%fused_computation.83 | convolution fusion | flops 2147483648 | bytes 13107200 | tf_op jit(solution)/shard_map/dot_general | solution.py:193
  31.8 39.6 %all-to-all-done = bf16[4,128,4096]{2,1,0:T(8,128)(2,1)} async-done(((bf16[4,128,4096]{2,1,0:T(8,128)(2,1)}), bf16[4,128,4096]{2,1,0:T(8,128)(2,1)}, u32[]{:S(2)}, u32[]{:S(2)}) %all-to-all-start) | async-done | bytes 4194336 | tf_op jit(solution)/shard_map/all_to_all | solution.py:190
  71.4 30.9 %all-gather.3.cloned.1.call-done = bf16[512,4608]{1,0:T(8,128)(2,1)} async-done(((bf16[128,4608]{1,0:T(8,128)(2,1)}), bf16[512,4608]{1,0:T(8,128)(2,1)}) %all-gather.3.cloned.1.call-update) | async-done | bytes 4718608 | tf_op jit(solution)/shard_map/all_gather | solution.py:157
  102.3 0.0 copy-start.8
  102.3 2.1 %convolution_bitcast_fusion.2 = f32[4,1,32,128]{3,2,0,1:T(8,128)S(1)} fusion(bf16[4,128,4608]{2,1,0:T(8,128)(2,1)} %bitcast.87, bf16[4,128,4096]{2,1,0:T(8,128)(2,1)} %all-to-all-done), kind=kOutput, calls=%fused_computation.13 | convolution fusion | flops 134217728 | bytes 2162688 | tf_op jit(solution)/shard_map/smd,nd->smn/dot_general | solution.py:198
  104.4 2.0 %convolution_bitcast_fusion.3 = f32[4,1,32,128]{3,2,0,1:T(8,128)S(1)} fusion(bf16[4,128,4608]{2,1,0:T(8,128)(2,1)} %bitcast.88, bf16[4,128,4096]{2,1,0:T(8,128)(2,1)} %all-to-all-done), kind=kOutput, calls=%fused_computation.14 | convolution fusion | flops 134217728 | bytes 2162688 | tf_op jit(solution)/shard_map/smd,nd->smn/dot_general | solution.py:198
  106.4 0.0 copy-done.8
  106.4 1.7 %convolution_bitcast_fusion.1 = f32[4,1,32,128]{3,2,0,1:T(8,128)S(1)} fusion(bf16[4,128,4608]{2,1,0:T(8,128)(2,1)S(1)} %bitcast.89, bf16[4,128,4096]{2,1,0:T(8,128)(2,1)} %all-to-all-done), kind=kOutput, calls=%fused_computation.12 | convolution fusion | flops 134217728 | bytes 2162688 | tf_op jit(solution)/shard_map/smd,nd->smn/dot_general | solution.py:198
  108.1 0.0 copy-start.4
  108.1 1.8 %convolution_bitcast_fusion = f32[4,1,32,128]{3,2,0,1:T(8,128)S(1)} fusion(bf16[4,128,4608]{2,1,0:T(8,128)(2,1)S(1)} %bitcast.90, bf16[4,128,4096]{2,1,0:T(8,128)(2,1)} %all-to-all-done), kind=kOutput, calls=%fused_computation.11 | convolution fusion | flops 134217728 | bytes 2162688 | tf_op jit(solution)/shard_map/smd,nd->smn/dot_general | solution.py:198
  110.0 1.6 collective-permute-start
  111.5 0.1 compare_select_fusion.diag_ref
  111.6 6.5 %collective-permute-done = f32[4,4,32,128]{3,2,0,1:T(8,128)S(1)} collective-permute-done((f32[4,4,32,128]{3,2,0,1:T(8,128)S(1)}, f32[4,4,32,128]{3,2,0,1:T(8,128)S(1)}, u32[]{:S(2)}, u32[]{:S(2)}) %collective-permute-start) | collective-permute-done | bytes 262176 | tf_op jit(solution)/shard_map/ppermute | solution.py:210
  118.1 0.1 multiply_convert_fusion
  118.2 0.2 fusion.1
  118.4 0.2 fusion.2
  118.6 0.2 fusion.3
  118.7 0.2 fusion.4
  118.9 0.1 pad_maximum_fusion.1
  119.0 0.8 copy.24
  119.8 3.5 %all-to-all-start.1 = ((bf16[4,128,512]{2,1,0:T(8,128)(2,1)}), bf16[4,128,512]{2,1,0:T(8,128)(2,1)S(1)}, u32[]{:S(2)}, u32[]{:S(2)}) async-start(bf16[4,128,512]{2,1,0:T(8,128)(2,1)} %bitcast.84), calls=%async_computation.1 | async-start | bytes 1048576 | tf_op jit(solution)/shard_map/all_to_all | solution.py:221
  123.3 0.0 copy-done.4
  123.3 0.0 copy-start
  123.3 3.4 %copy-done = bf16[256,32,512]{2,1,0:T(8,128)(2,1)S(1)} copy-done((bf16[256,32,512]{2,1,0:T(8,128)(2,1)S(1)}, bf16[256,32,512]{2,1,0:T(8,128)(2,1)}, u32[]{:S(2)}) %copy-start) | copy-done | bytes 8388632
  126.7 0.0 copy-start.1
  126.7 3.4 %copy-done.1 = bf16[256,32,512]{2,1,0:T(8,128)(2,1)S(1)} copy-done((bf16[256,32,512]{2,1,0:T(8,128)(2,1)S(1)}, bf16[256,32,512]{2,1,0:T(8,128)(2,1)}, u32[]{:S(2)}) %copy-start.1) | copy-done | bytes 8388632
  130.1 0.0 copy-start.5
  130.1 0.9 copy-done.5
  131.0 19.6 %attend_cache.1 = (f32[256,4096]{1,0:T(8,128)S(1)}, f32[256,32]{1,0:T(8,128)S(1)}) custom-call(bf16[256,4096]{1,0:T(8,128)(2,1)S(1)} %copy-done.4, bf16[256,512]{1,0:T(8,128)(2,1)S(1)} %copy-done.5, bf16[256,32,512]{2,1,0:T(8,128)(2,1)S(1)} %copy-done, bf16[256,32,512]{2,1,0:T(8,128)(2,1)S(1)} %copy-done.1, f32[16,1,512]{2,1,0:T(1,128)S(1)} %compare_select_fusion.1.col_ref, ...), custom_call_target="tpu_custom_call" | custom-call | flops 2147483648 | bytes 23068672 | tf_op jit(solution)/shard_map/attend_cache/pallas_call | solution.py:58
  150.6 0.0 copy-start.2
  150.6 1.9 %copy-done.2 = f32[256,4096]{1,0:T(8,128)} copy-done((f32[256,4096]{1,0:T(8,128)}, f32[256,4096]{1,0:T(8,128)S(1)}, u32[]{:S(2)}) %copy-start.2) | copy-done | bytes 4194328
  152.5 0.0 copy-start.6
  152.5 0.7 copy-done.6
  153.2 0.1 fusion.9.place_ref
  153.3 0.0 all-to-all-done.1
  153.3 0.0 copy-start.3
  153.3 2.2 %copy-done.3 = f32[256,4096]{1,0:T(8,128)S(1)} copy-done((f32[256,4096]{1,0:T(8,128)S(1)}, f32[256,4096]{1,0:T(8,128)}, u32[]{:S(2)}) %copy-start.3) | copy-done | bytes 4194328
  155.5 0.0 copy-start.7
  155.5 0.9 copy-done.7
  156.4 2.8 %finish_rows.1 = (bf16[256,512]{1,0:T(8,128)(2,1)}, bf16[256,4096]{1,0:T(8,128)(2,1)}) custom-call(bf16[512,512]{1,0:T(8,128)(2,1)S(1)} %bitcast.82, bf16[256,512]{1,0:T(8,128)(2,1)S(1)} %fusion.9.place_ref, f32[256,512]{1,0:T(8,128)S(1)} %fusion.21.base_ref, f32[256,4096]{1,0:T(8,128)S(1)} %copy-done.3, f32[256,32]{1,0:T(8,128)S(1)} %copy-done.7), custom_call_target="tpu_custom_call" | custom-call | flops 268435456 | bytes 6291456 | tf_op jit(solution)/shard_map/finish_rows/pallas_call | solution.py:105
  (9 shorter events, 0.1 us)
Async XLA Ops:
  7.2 95.1 %all-gather.3.cloned.1.call-start = ((), (), s32[]{:S(2)}) async-start(), calls=%async_computation.2 | async-start | bytes 5898240 | tf_op jit(solution)/shard_map/all_gather | solution.py:157
  17.3 6.3 %copy-start.9 = (s32[1,256]{1,0:T(1,128)S(1)}, s32[1,256]{1,0:T(1,128)}, u32[]{:S(2)}) copy-start(s32[1,256]{1,0:T(1,128)} %param.19) | copy-start | bytes 3076
  17.3 54.1 %all-to-all-start = ((bf16[4,128,4096]{2,1,0:T(8,128)(2,1)}), bf16[4,128,4096]{2,1,0:T(8,128)(2,1)}, u32[]{:S(2)}, u32[]{:S(2)}) async-start(bf16[4,128,4096]{2,1,0:T(8,128)(2,1)} %bitcast.83), calls=%async_computation | async-start | bytes 8388608 | tf_op jit(solution)/shard_map/all_to_all | solution.py:190
  102.3 4.1 %copy-start.8 = (bf16[512,4608]{1,0:T(8,128)(2,1)S(1)}, bf16[512,4608]{1,0:T(8,128)(2,1)}, u32[]{:S(2)}) copy-start(bf16[512,4608]{1,0:T(8,128)(2,1)} %all-gather.3.cloned.1.call-done) | copy-start | bytes 14155780
  108.1 15.2 %copy-start.4 = (bf16[256,4096]{1,0:T(8,128)(2,1)S(1)}, bf16[256,4096]{1,0:T(8,128)(2,1)}, u32[]{:S(2)}) copy-start(bf16[256,4096]{1,0:T(8,128)(2,1)} %q_ref.1) | copy-start | bytes 6291460
  110.0 8.2 %collective-permute-start = (f32[4,4,32,128]{3,2,0,1:T(8,128)S(1)}, f32[4,4,32,128]{3,2,0,1:T(8,128)S(1)}, u32[]{:S(2)}, u32[]{:S(2)}) collective-permute-start(f32[4,4,32,128]{3,2,0,1:T(8,128)S(1)} %pad_maximum_fusion.2), channel_id=1, source_target_pairs={{0,1},{1,0},{2,3},{3,2},{4,5},{5,4},{6,7},{7,6},{8,9},{9,8},{10,11... | collective-permute-start | bytes 786440 | tf_op jit(solution)/shard_map/ppermute | solution.py:210
  119.8 33.5 %all-to-all-start.1 = ((bf16[4,128,512]{2,1,0:T(8,128)(2,1)}), bf16[4,128,512]{2,1,0:T(8,128)(2,1)S(1)}, u32[]{:S(2)}, u32[]{:S(2)}) async-start(bf16[4,128,512]{2,1,0:T(8,128)(2,1)} %bitcast.84), calls=%async_computation.1 | async-start | bytes 1048576 | tf_op jit(solution)/shard_map/all_to_all | solution.py:221
  123.3 3.4 %copy-start = (bf16[256,32,512]{2,1,0:T(8,128)(2,1)S(1)}, bf16[256,32,512]{2,1,0:T(8,128)(2,1)}, u32[]{:S(2)}) copy-start(bf16[256,32,512]{2,1,0:T(8,128)(2,1)} %k_ref.1) | copy-start | bytes 25165828
  126.7 3.4 %copy-start.1 = (bf16[256,32,512]{2,1,0:T(8,128)(2,1)S(1)}, bf16[256,32,512]{2,1,0:T(8,128)(2,1)}, u32[]{:S(2)}) copy-start(bf16[256,32,512]{2,1,0:T(8,128)(2,1)} %v_ref.1) | copy-start | bytes 25165828
  130.1 0.9 copy-start.5
  150.6 1.9 %copy-start.2 = (f32[256,4096]{1,0:T(8,128)}, f32[256,4096]{1,0:T(8,128)S(1)}, u32[]{:S(2)}) copy-start(f32[256,4096]{1,0:T(8,128)S(1)} %get-tuple-element.4.ctx_ref) | copy-start | bytes 12582916
  152.5 0.7 copy-start.6
  153.3 2.2 %copy-start.3 = (f32[256,4096]{1,0:T(8,128)S(1)}, f32[256,4096]{1,0:T(8,128)}, u32[]{:S(2)}) copy-start(f32[256,4096]{1,0:T(8,128)} %copy-done.2) | copy-start | bytes 12582916
  155.5 0.9 copy-start.7
Sparse Core Ops, SparseCore 0:
  10.1 92.0 all-gather.2
